TPU v7x, 32 devices: a whole 2x2x4 slice. The times are simulated.
32 devices in a mesh: space: 8 (over z, x), member: 4 (over y, core).
Axes of the slice: x: 2, y: 2, z: 4, core: 2. Of those that a mesh axis runs over, the one named last changes fastest.
Arguments:
- fields: float32 [8, 16, 128, 256], P('member', 'space'), may hold values from -6 to 6
- velocity: float32 [16, 128, 256], P('space'), may hold values from 0.2 to 0.6
- building: int32 [16, 128, 256], P('space'), may hold values 0 or 1
- inflow_table: float32 [32, 128, 256], replicated, may hold values from -6 to 6
- inflow_index: int32 [8], P('member'), may hold values from 0 to 31
Outputs:
- fields_now: float32 [8, 16, 128, 256], P('member', 'space')
- r_factor: float32 [8, 8], replicated
All inputs are finite; a program needn't handle non-finite values. No bound on the sum of `building` on one device may be relied on, other than what follows from the above.
Results may differ from a plain program's by a relative error of at most 0.0003.
Values may be sent and summed in bfloat16 or wider, within the bound.
A program may use at most 64 MiB of HBM per device.

v0:
```python
import jax
import jax.numpy as jnp
from jax import lax
from jax.sharding import PartitionSpec as P

STEPS = 2
kappa_rate = 0.05
shrink_weight = 0.1
contract_dims = (((1,), (1,)), ((), ()))


def extended_2(block, sides, width):
    for axis, dim in sides:
        count = lax.axis_size(axis)
        forward = [(i, i + 1) for i in range(count - 1)]
        backward = [(target, source) for source, target in forward]
        low = lax.ppermute(
            lax.slice_in_dim(block, block.shape[dim] - width, None, axis=dim), axis, forward
        )
        high = lax.ppermute(lax.slice_in_dim(block, 0, width, axis=dim), axis, backward)
        block = jnp.concatenate([low, block, high], axis=dim)
    return block


def from_behind(block, axis, distance):
    devices = range(lax.axis_size(axis))
    route = [((i - distance) % len(devices), i) for i in devices]
    return lax.ppermute(block, axis, route)


def advance(extended, fluid_cells, courant):
    upwind = extended[:, :-2]
    centre = extended[:, 1:-1]
    downwind = extended[:, 2:]
    in_plane = (
        jnp.roll(centre, 1, 2)
        + jnp.roll(centre, -1, 2)
        + jnp.roll(centre, 1, 3)
        + jnp.roll(centre, -1, 3)
    )
    return fluid_cells * (
        centre
        + courant * (upwind - centre)
        + kappa_rate * (upwind + downwind + in_plane - 6.0 * centre)
    )


def local(fields, velocity, building, inflow_table, inflow_index):
    mem_dev = fields.shape[0]
    slab_depth = fields.shape[1]
    plane_rows = fields.shape[2]
    plane_cols = fields.shape[3]
    patterns = inflow_table.shape[0]
    fluid_cells = (1 - building).astype(jnp.float32)
    pattern_pick = (inflow_index[:, None] == jnp.arange(patterns, dtype=jnp.int32)[None, :]).astype(
        jnp.float32
    )
    inflow_plane = jnp.dot(
        pattern_pick,
        inflow_table.reshape(patterns, plane_rows * plane_cols),
        precision=lax.Precision.HIGHEST,
        preferred_element_type=jnp.float32,
    ).reshape(mem_dev, plane_rows, plane_cols)
    at_inflow = lax.axis_index("space") == 0
    fields_now = fields
    for sweep_index in range(STEPS):
        extended = extended_2(fields_now, (("space", 1),), 1)
        extended = extended.at[:, 0].set(jnp.where(at_inflow, inflow_plane, extended[:, 0]))
        fields_now = advance(extended, fluid_cells, velocity)
    groups = lax.axis_size("member")
    all_members = mem_dev * groups
    member_sum = jnp.sum(fields_now, 0)
    ensemble_mean = (
        lax.psum(member_sum.astype(jnp.bfloat16), "member").astype(jnp.float32) / all_members
    )
    anomaly = (
        (fields_now - ensemble_mean)
        .astype(jnp.bfloat16)
        .reshape(mem_dev, slab_depth * plane_rows * plane_cols)
    )
    my_group = lax.axis_index("member")
    cells_all = slab_depth * lax.axis_size("space") * plane_rows * plane_cols
    empty_rows = jnp.zeros((mem_dev, all_members), jnp.float32)

    def place(gram_tile, panel_piece, first_row):
        gram_block = lax.dot_general(
            anomaly, panel_piece, contract_dims, preferred_element_type=jnp.float32
        )
        return lax.dynamic_update_slice(
            gram_tile, gram_block, (jnp.int32(0), jnp.asarray(first_row))
        )

    gram_tile = place(empty_rows, anomaly, my_group * mem_dev)

    def turn(sweep_index, loop_state):
        tile_now, panel_held = loop_state
        panel_held = from_behind(panel_held, "member", 1)
        source = (my_group - sweep_index) % groups
        return (place(tile_now, panel_held, source * mem_dev), panel_held)

    gram_tile, panel_held = lax.fori_loop(1, groups, turn, (gram_tile, anomaly))
    gram_tile = gram_tile / cells_all
    summed = lax.psum(gram_tile, "space")
    gram_full = lax.all_gather(summed, "member", axis=0, tiled=True)
    r_factor = jnp.linalg.cholesky(
        gram_full + shrink_weight * jnp.eye(all_members, dtype=jnp.float32)
    ).T
    return (fields_now, r_factor)


def solution(mesh):
    placed = (
        P("member", "space", None, None),
        P("space", None, None),
        P("space", None, None),
        P(),
        P("member"),
    )
    return jax.shard_map(
        local,
        mesh=mesh,
        in_specs=placed,
        out_specs=(P("member", "space", None, None), P()),
        check_vma=False,
    )
```

profile of v0, /device:TPU:0, one launch (start us, length us, event | category | flops | bytes accessed | tf_op | source)
XLA Modules:
  0.0 151.2 jit_solution(6526579312249673913)
XLA Ops:
  7.2 1.4 copy.24
  8.7 0.2 fusion.33
  8.9 4.9 %collective-permute-start.1 = (f32[2,1,128,256]{3,0,2,1:T(2,128)S(1)}, f32[2,1,128,256]{3,0,2,1:T(2,128)S(1)}, u32[]{:S(2)}, u32[]{:S(2)}) collective-permute-start(f32[2,1,128,256]{3,0,2,1:T(2,128)S(1)} %get-tuple-element.196), channel_id=1, source_target_pairs={{0,4},{4,8},{8,12},{12,16},{16,20},{20,24},{24,28},{1,5},{5,9},{9,... | collective-permute-start | bytes 786440 | tf_op jit(solution)/shard_map/ppermute | solution.py:17
  13.7 1.3 collective-permute-start.2
  15.0 1.0 subtract_convert_fusion.1
  16.0 8.9 %collective-permute-done.1 = f32[2,1,128,256]{3,0,2,1:T(2,128)S(1)} collective-permute-done((f32[2,1,128,256]{3,0,2,1:T(2,128)S(1)}, f32[2,1,128,256]{3,0,2,1:T(2,128)S(1)}, u32[]{:S(2)}, u32[]{:S(2)}) %collective-permute-start.1) | collective-permute-done | bytes 262176 | tf_op jit(solution)/shard_map/ppermute | solution.py:17
  24.9 0.5 pad_maximum_fusion
  25.4 6.0 %bitcast_dynamic-update-slice_fusion.1 = (f32[2,4,128,256]{3,0,2,1:T(2,128)S(1)}, f32[2,128,256]{2,0,1:T(2,128)S(1)}) fusion(f32[2,4,128,256]{3,0,2,1:T(2,128)S(1)} %pad_maximum_fusion, f32[2,1,128,256]{3,0,2,1:T(2,128)S(1)} %collective-permute-done.1, pred[]{:T(512)S(6)} %eq.25, s32[2]{0:T(128)S(1)} %copy-done.1, f32[4,8,128,256]{3,2,1,0:T(8,128)} %bitcast.51), kind=kOutput, calls=%fused_computation.27 | convolution fusion | flops 25231424 | bytes 4981249 | tf_op jit(solution)/shard_map/dot_general | solution.py:58
  31.4 0.7 fusion.31
  32.1 0.3 fusion.29
  32.3 0.3 fusion.30
  32.7 1.9 %fusion.15 = f32[2,2,128,256]{3,0,2,1:T(2,128)S(1)} fusion(f32[2,2,128,1]{3,0,2,1:T(2,128)S(1)} %get-tuple-element.191, f32[2,2,128,255]{3,0,2,1:T(2,128)S(1)} %get-tuple-element.193, f32[2,2,128,255]{3,0,2,1:T(2,128)S(1)} %get-tuple-element.192, f32[2,2,128,1]{3,0,2,1:T(2,128)S(1)} %get-tuple-element.190, f32[2,2,1,256]{3,0,2,1:T(2,128)S(1)} %get-tuple-element.187, ...), kind=kLoop, calls=%fused_computation.23 | loop fusion | flops 2228224 | bytes 4718592 | tf_op jit(solution)/shard_map/mul | solution.py:41
  34.7 0.2 fusion.32
  34.8 4.4 %collective-permute-start.3 = (f32[2,1,128,256]{3,0,2,1:T(2,128)S(1)}, f32[2,1,128,256]{3,0,2,1:T(2,128)S(1)}, u32[]{:S(2)}, u32[]{:S(2)}) collective-permute-start(f32[2,1,128,256]{3,0,2,1:T(2,128)S(1)} %get-tuple-element.194), channel_id=1, source_target_pairs={{0,4},{4,8},{8,12},{12,16},{16,20},{20,24},{24,28},{1,5},{5,9},{9,... | collective-permute-start | bytes 786440 | tf_op jit(solution)/shard_map/ppermute | solution.py:17
  39.3 1.5 collective-permute-start.4
  40.7 3.2 %collective-permute-done.3 = f32[2,1,128,256]{3,0,2,1:T(2,128)S(1)} collective-permute-done((f32[2,1,128,256]{3,0,2,1:T(2,128)S(1)}, f32[2,1,128,256]{3,0,2,1:T(2,128)S(1)}, u32[]{:S(2)}, u32[]{:S(2)}) %collective-permute-start.3) | collective-permute-done | bytes 262176 | tf_op jit(solution)/shard_map/ppermute | solution.py:17
  43.9 5.9 %collective-permute-done.4 = f32[2,1,128,256]{3,0,2,1:T(2,128)S(1)} collective-permute-done((f32[2,1,128,256]{3,0,2,1:T(2,128)S(1)}, f32[2,1,128,256]{3,0,2,1:T(2,128)S(1)}, u32[]{:S(2)}, u32[]{:S(2)}) %collective-permute-start.4) | collective-permute-done | bytes 262176 | tf_op jit(solution)/shard_map/ppermute | solution.py:20
  49.8 0.5 pad_maximum_fusion.1
  50.3 0.2 bitcast_dynamic-update-slice_fusion
  50.4 0.7 fusion.27
  51.1 0.3 fusion.25
  51.4 0.3 fusion.26
  51.8 3.2 %fusion.22 = (bf16[2,128,256]{2,1,0:T(8,128)(2,1)}, f32[2,2,128,256]{3,0,2,1:T(2,128)S(1)}) fusion(f32[2,2,128,1]{3,0,2,1:T(2,128)S(1)} %get-tuple-element.183, f32[2,2,128,255]{3,0,2,1:T(2,128)S(1)} %get-tuple-element.185, f32[2,2,128,255]{3,0,2,1:T(2,128)S(1)} %get-tuple-element.184, f32[2,2,128,1]{3,0,2,1:T(2,128)S(1)} %get-tuple-element.182, ...), kind=kLoop, calls=%fused_computation.44 | loop fusion | flops 2293760 | bytes 4849664 | tf_op jit(solution)/shard_map/reduce_sum | solution.py:72
  55.0 35.5 %all-reduce.2.cloned.1.call-done = bf16[2,128,256]{2,1,0:T(8,128)(2,1)} async-done(((bf16[2,128,256]{2,1,0:T(8,128)(2,1)}), bf16[2,128,256]{2,1,0:T(8,128)(2,1)}) %all-reduce.2.cloned.1.call-update) | async-done | bytes 131088 | tf_op jit(solution)/shard_map/psum | solution.py:74
  90.5 0.9 convert_multiply_fusion
  91.4 0.3 subtract_convert_fusion
  91.7 0.9 convolution_bitcast_fusion
  92.5 0.2 copy.52
  92.8 0.1 dynamic_update_slice.13
  92.9 21.1 %while.19 = (s32[]{:T(128)}, f32[2,8]{1,0:T(2,128)S(1)}, bf16[2,65536]{1,0:T(2,128)(2,1)S(1)}, bf16[2,65536]{1,0:T(2,128)(2,1)S(1)}, s32[]{:T(128)}, /*index=5*/...) while((s32[]{:T(128)}, f32[2,8]{1,0:T(2,128)S(1)}, ...), condition=%wide.region_3.4_spmd, body=%wide.region_2.3_spmd.sunk | while | flops 524306 | bytes 2097520 | solution.py:101
  93.0 5.8 %collective-permute-done = bf16[2,65536]{1,0:T(2,128)(2,1)S(1)} collective-permute-done((bf16[2,65536]{1,0:T(2,128)(2,1)S(1)}, bf16[2,65536]{1,0:T(2,128)(2,1)S(1)}, u32[]{:S(2)}, u32[]{:S(2)}) %collective-permute-start) | collective-permute-done | bytes 262176 | tf_op jit(solution)/shard_map/while/body/eval_jaxpr/ppermute | solution.py:28
  98.8 0.8 fusion.44
  99.5 0.2 dynamic_update_slice.15
  99.7 0.2 copy.58
  100.0 5.8 %collective-permute-done = bf16[2,65536]{1,0:T(2,128)(2,1)S(1)} collective-permute-done((bf16[2,65536]{1,0:T(2,128)(2,1)S(1)}, bf16[2,65536]{1,0:T(2,128)(2,1)S(1)}, u32[]{:S(2)}, u32[]{:S(2)}) %collective-permute-start) | collective-permute-done | bytes 262176 | tf_op jit(solution)/shard_map/while/body/eval_jaxpr/ppermute | solution.py:28
  105.8 0.8 fusion.44
  106.6 0.2 dynamic_update_slice.15
  106.8 0.2 copy.58
  107.1 5.8 %collective-permute-done = bf16[2,65536]{1,0:T(2,128)(2,1)S(1)} collective-permute-done((bf16[2,65536]{1,0:T(2,128)(2,1)S(1)}, bf16[2,65536]{1,0:T(2,128)(2,1)S(1)}, u32[]{:S(2)}, u32[]{:S(2)}) %collective-permute-start) | collective-permute-done | bytes 262176 | tf_op jit(solution)/shard_map/while/body/eval_jaxpr/ppermute | solution.py:28
  112.8 0.8 fusion.44
  113.6 0.2 dynamic_update_slice.15
  113.8 0.2 copy.58
  114.0 0.8 copy.32
  114.9 21.3 %psum.15 = f32[2,8]{1,0:T(2,128)S(1)} all-reduce(f32[2,8]{1,0:T(2,128)S(1)} %broadcast_multiply_fusion), channel_id=1, replica_groups=mesh['space'=8,'member'=4] {'space'}, use_global_device_ids=true, to_apply=%region_4.5 | all-reduce | flops 16 | bytes 128 | tf_op jit(solution)/shard_map/psum | solution.py:103
  136.2 5.1 %all-gather = f32[4,2,8]{2,1,0:T(2,128)S(1)} all-gather(f32[1,2,8]{2,1,0:T(2,128)S(1)} %bitcast.55), channel_id=1, replica_groups=mesh['space'=8,'member'=4] {'member'}, dimensions={0}, use_global_device_ids=true | all-gather | bytes 320 | tf_op jit(solution)/shard_map/all_gather | solution.py:104
  141.4 0.7 cholesky.19
  142.3 0.7 compare_reduce_fusion
  143.1 1.3 select_bitcast_fusion
  (20 shorter events, 0.6 us)
Async XLA Ops:
  7.2 18.2 %copy-start.1 = (s32[2]{0:T(128)S(1)}, s32[2]{0:T(128)}, u32[]{:S(2)}) copy-start(s32[2]{0:T(128)} %param.15) | copy-start | bytes 28
  7.2 83.3 %all-reduce.2.cloned.1.call-start = ((), (), s32[]{:S(2)}) async-start(), calls=%async_computation | async-start | bytes 262144 | tf_op jit(solution)/shard_map/psum | solution.py:74
  8.9 16.0 %collective-permute-start.1 = (f32[2,1,128,256]{3,0,2,1:T(2,128)S(1)}, f32[2,1,128,256]{3,0,2,1:T(2,128)S(1)}, u32[]{:S(2)}, u32[]{:S(2)}) collective-permute-start(f32[2,1,128,256]{3,0,2,1:T(2,128)S(1)} %get-tuple-element.196), channel_id=1, source_target_pairs={{0,4},{4,8},{8,12},{12,16},{16,20},{20,24},{24,28},{1,5},{5,9},{9,... | collective-permute-start | bytes 786440 | tf_op jit(solution)/shard_map/ppermute | solution.py:17
  13.7 11.2 %collective-permute-start.2 = (f32[2,1,128,256]{3,0,2,1:T(2,128)S(1)}, f32[2,1,128,256]{3,0,2,1:T(2,128)S(1)}, u32[]{:S(2)}, u32[]{:S(2)}) collective-permute-start(f32[2,1,128,256]{3,0,2,1:T(2,128)S(1)} %get-tuple-element.197), channel_id=1, source_target_pairs={{4,0},{8,4},{12,8},{16,12},{20,16},{24,20},{28,24},{5,1},{9,5},{13... | collective-permute-start | bytes 786440 | tf_op jit(solution)/shard_map/ppermute | solution.py:20
  25.4 7.3 %copy-start = (f32[2,128,256]{2,1,0:T(8,128)S(1)}, f32[2,128,256]{2,1,0:T(8,128)}, u32[]{:S(2)}) copy-start(f32[2,128,256]{2,1,0:T(8,128)} %param.12) | copy-start | bytes 786436
  34.8 9.1 %collective-permute-start.3 = (f32[2,1,128,256]{3,0,2,1:T(2,128)S(1)}, f32[2,1,128,256]{3,0,2,1:T(2,128)S(1)}, u32[]{:S(2)}, u32[]{:S(2)}) collective-permute-start(f32[2,1,128,256]{3,0,2,1:T(2,128)S(1)} %get-tuple-element.194), channel_id=1, source_target_pairs={{0,4},{4,8},{8,12},{12,16},{16,20},{20,24},{24,28},{1,5},{5,9},{9,... | collective-permute-start | bytes 786440 | tf_op jit(solution)/shard_map/ppermute | solution.py:17
  39.3 10.5 %collective-permute-start.4 = (f32[2,1,128,256]{3,0,2,1:T(2,128)S(1)}, f32[2,1,128,256]{3,0,2,1:T(2,128)S(1)}, u32[]{:S(2)}, u32[]{:S(2)}) collective-permute-start(f32[2,1,128,256]{3,0,2,1:T(2,128)S(1)} %get-tuple-element.195), channel_id=1, source_target_pairs={{4,0},{8,4},{12,8},{16,12},{20,16},{24,20},{28,24},{5,1},{9,5},{13... | collective-permute-start | bytes 786440 | tf_op jit(solution)/shard_map/ppermute | solution.py:20
  92.9 5.8 %collective-permute-start = (bf16[2,65536]{1,0:T(2,128)(2,1)S(1)}, bf16[2,65536]{1,0:T(2,128)(2,1)S(1)}, u32[]{:S(2)}, u32[]{:S(2)}) collective-permute-start(bf16[2,65536]{1,0:T(2,128)(2,1)S(1)} %get-tuple-element.244), channel_id=1, source_target_pairs={{3,0},{0,1},{1,2},{2,3},{7,4},{4,5},{5,6},{6,7},{11,8},{8,9},{9,10... | collective-permute-start | bytes 786440 | tf_op jit(solution)/shard_map/while/body/eval_jaxpr/ppermute | solution.py:28
  99.9 5.8 %collective-permute-start = (bf16[2,65536]{1,0:T(2,128)(2,1)S(1)}, bf16[2,65536]{1,0:T(2,128)(2,1)S(1)}, u32[]{:S(2)}, u32[]{:S(2)}) collective-permute-start(bf16[2,65536]{1,0:T(2,128)(2,1)S(1)} %get-tuple-element.244), channel_id=1, source_target_pairs={{3,0},{0,1},{1,2},{2,3},{7,4},{4,5},{5,6},{6,7},{11,8},{8,9},{9,10... | collective-permute-start | bytes 786440 | tf_op jit(solution)/shard_map/while/body/eval_jaxpr/ppermute | solution.py:28
  107.0 5.8 %collective-permute-start = (bf16[2,65536]{1,0:T(2,128)(2,1)S(1)}, bf16[2,65536]{1,0:T(2,128)(2,1)S(1)}, u32[]{:S(2)}, u32[]{:S(2)}) collective-permute-start(bf16[2,65536]{1,0:T(2,128)(2,1)S(1)} %get-tuple-element.244), channel_id=1, source_target_pairs={{3,0},{0,1},{1,2},{2,3},{7,4},{4,5},{5,6},{6,7},{11,8},{8,9},{9,10... | collective-permute-start | bytes 786440 | tf_op jit(solution)/shard_map/while/body/eval_jaxpr/ppermute | solution.py:28
Sparse Core Ops, SparseCore 0:
  55.1 35.3 all-reduce.1
where the time goes:
time: 151 us
  waiting for transfers between devices  70.7 us (47%)
  blocking collectives  26.4 us (17%)
  between operations  14.3 us (9%)
  starting transfers between devices  12.2 us (8%)
  other arithmetic  11.2 us (7%)
  matrix products  9.16 us (6%)
  local copies, waits for them, and re-layouts  7.04 us (5%)
    psum x1, waiting for transfers between devices, local(): lax.psum(member_sum.astype(jnp.bfloat16), 'member').astype(jnp.float32)  35.5 us
    psum x1, blocking collectives, local(): summed = lax.psum(gram_tile, 'space')  21.3 us
    ppermute x3, waiting for transfers between devices, from_behind(): return lax.ppermute(block, axis, route)  17.3 us
    ppermute x2, waiting for transfers between devices, extended_2(): lax.ppermute(lax.slice_in_dim(block, block.shape[dim] - width, None, axis...  12 us
    ppermute x2, starting transfers between devices, extended_2(): lax.ppermute(lax.slice_in_dim(block, block.shape[dim] - width, None, axis...  9.26 us
    dot_general x1, matrix products, local(): jnp.dot(pattern_pick, inflow_table.reshape(patterns, plane_rows * plane_c...  5.97 us
    ppermute x2, waiting for transfers between devices, extended_2(): lax.ppermute(lax.slice_in_dim(block, 0, width, axis=dim), axis, backward)  5.88 us
    all_gather x1, blocking collectives, local(): gram_full = lax.all_gather(summed, 'member', axis=0, tiled=True)  5.06 us
  transfers between devices with their start and end apart: 8, of which 7 were waited for; matrix products, arithmetic and copies ran while one was open for 1% of the time, Pallas kernels for 0%

commit v1 on v0

--- a/solution.py
+++ b/solution.py
@@ -100,7 +100,9 @@
 
     gram_tile, panel_held = lax.fori_loop(1, groups, turn, (gram_tile, anomaly))
     gram_tile = gram_tile / cells_all
-    summed = lax.psum(gram_tile, "space")
+    summed = gram_tile
+    for hop in (1, 2, 4):
+        summed = summed + lax.ppermute(summed, "space", [(dev, dev ^ hop) for dev in range(8)])
     gram_full = lax.all_gather(summed, "member", axis=0, tiled=True)
     r_factor = jnp.linalg.cholesky(
         gram_full + shrink_weight * jnp.eye(all_members, dtype=jnp.float32)

time: 151 us -> 141 us (0.934)
  blocking collectives: 26.4 us -> 5.06 us
  starting transfers between devices: 12.2 us -> 17.7 us
  waiting for transfers between devices: 70.7 us -> 76.1 us
    psum x1 -> x0, blocking collectives: 21.3 us -> none  [local(): summed = lax.psum(gram_tile, 'space')]
    ppermute x0 -> x3, starting transfers between devices: none -> 5.43 us  [local(): lax.ppermute(summed, 'space', [(dev, dev ^ hop) for dev in range(8)])]
    ppermute x0 -> x3, waiting for transfers between devices: none -> 5.4 us  [local(): lax.ppermute(summed, 'space', [(dev, dev ^ hop) for dev in range(8)])]
  transfers between devices with their start and end apart: 8 -> 11, of which waited for: 7 -> 10; matrix products, arithmetic and copies ran while one was open for 1% -> 1% of each run, Pallas kernels for 0% -> 0%
where the time goes in v1:
time: 141 us
  waiting for transfers between devices  76.1 us (54%)
  starting transfers between devices  17.7 us (13%)
  between operations  14.3 us (10%)
  other arithmetic  11.1 us (8%)
  matrix products  9.16 us (6%)
  local copies, waits for them, and re-layouts  7.04 us (5%)
  blocking collectives  5.06 us (4%)
    psum x1, waiting for transfers between devices, local(): lax.psum(member_sum.astype(jnp.bfloat16), 'member').astype(jnp.float32)  35.5 us
    ppermute x3, waiting for transfers between devices, from_behind(): return lax.ppermute(block, axis, route)  17.3 us
    ppermute x2, waiting for transfers between devices, extended_2(): lax.ppermute(lax.slice_in_dim(block, block.shape[dim] - width, None, axis...  12 us
    ppermute x2, starting transfers between devices, extended_2(): lax.ppermute(lax.slice_in_dim(block, block.shape[dim] - width, None, axis...  9.26 us
    dot_general x1, matrix products, local(): jnp.dot(pattern_pick, inflow_table.reshape(patterns, plane_rows * plane_c...  5.97 us
    ppermute x2, waiting for transfers between devices, extended_2(): lax.ppermute(lax.slice_in_dim(block, 0, width, axis=dim), axis, backward)  5.88 us
    ppermute x3, starting transfers between devices, local(): lax.ppermute(summed, 'space', [(dev, dev ^ hop) for dev in range(8)])  5.43 us
    ppermute x3, waiting for transfers between devices, local(): lax.ppermute(summed, 'space', [(dev, dev ^ hop) for dev in range(8)])  5.4 us
  transfers between devices with their start and end apart: 11, of which 10 were waited for; matrix products, arithmetic and copies ran while one was open for 1% of the time, Pallas kernels for 0%

profile of v1, /device:TPU:0, one launch (start us, length us, event | category | flops | bytes accessed | tf_op | source)
XLA Modules:
  0.0 140.6 jit_solution(3690197124955204420)
XLA Ops:
  7.2 1.4 %copy.24 = f32[2,2,128,256]{3,0,2,1:T(2,128)S(1)} copy(f32[2,2,128,256]{3,2,1,0:T(8,128)} %param.11) | data formatting | bytes 1048576 | tf_op args[0]
  8.9 4.9 %collective-permute-start.1 = (f32[2,1,128,256]{3,0,2,1:T(2,128)S(1)}, f32[2,1,128,256]{3,0,2,1:T(2,128)S(1)}, u32[]{:S(2)}, u32[]{:S(2)}) collective-permute-start(f32[2,1,128,256]{3,0,2,1:T(2,128)S(1)} %get-tuple-element.196), channel_id=1, source_target_pairs={{0,4},{4,8},{8,12},{12,16},{16,20},{20,24},{24,28},{1,5},{5,9},{9,... | collective-permute-start | bytes 786440 | tf_op jit(solution)/shard_map/ppermute | solution.py:17
  13.7 1.3 collective-permute-start.2
  15.0 1.0 subtract_convert_fusion.1
  16.0 8.9 %collective-permute-done.1 = f32[2,1,128,256]{3,0,2,1:T(2,128)S(1)} collective-permute-done((f32[2,1,128,256]{3,0,2,1:T(2,128)S(1)}, f32[2,1,128,256]{3,0,2,1:T(2,128)S(1)}, u32[]{:S(2)}, u32[]{:S(2)}) %collective-permute-start.1) | collective-permute-done | bytes 262176 | tf_op jit(solution)/shard_map/ppermute | solution.py:17
  24.9 0.5 pad_maximum_fusion
  25.4 6.0 %bitcast_dynamic-update-slice_fusion.1 = (f32[2,4,128,256]{3,0,2,1:T(2,128)S(1)}, f32[2,128,256]{2,0,1:T(2,128)S(1)}) fusion(f32[2,4,128,256]{3,0,2,1:T(2,128)S(1)} %pad_maximum_fusion, f32[2,1,128,256]{3,0,2,1:T(2,128)S(1)} %collective-permute-done.1, pred[]{:T(512)S(6)} %eq.25, s32[2]{0:T(128)S(1)} %copy-done.1, f32[4,8,128,256]{3,2,1,0:T(8,128)} %bitcast.52), kind=kOutput, calls=%fused_computation.27 | convolution fusion | flops 25231424 | bytes 4981249 | tf_op jit(solution)/shard_map/dot_general | solution.py:58
  31.4 0.7 fusion.32
  32.1 0.3 fusion.30
  32.3 0.3 fusion.31
  32.7 1.9 %fusion.15 = f32[2,2,128,256]{3,0,2,1:T(2,128)S(1)} fusion(f32[2,2,128,1]{3,0,2,1:T(2,128)S(1)} %get-tuple-element.191, f32[2,2,128,255]{3,0,2,1:T(2,128)S(1)} %get-tuple-element.193, f32[2,2,128,255]{3,0,2,1:T(2,128)S(1)} %get-tuple-element.192, f32[2,2,128,1]{3,0,2,1:T(2,128)S(1)} %get-tuple-element.190, f32[2,2,1,256]{3,0,2,1:T(2,128)S(1)} %get-tuple-element.187, ...), kind=kLoop, calls=%fused_computation.23 | loop fusion | flops 2228224 | bytes 4718592 | tf_op jit(solution)/shard_map/mul | solution.py:41
  34.8 4.4 %collective-permute-start.3 = (f32[2,1,128,256]{3,0,2,1:T(2,128)S(1)}, f32[2,1,128,256]{3,0,2,1:T(2,128)S(1)}, u32[]{:S(2)}, u32[]{:S(2)}) collective-permute-start(f32[2,1,128,256]{3,0,2,1:T(2,128)S(1)} %get-tuple-element.194), channel_id=1, source_target_pairs={{0,4},{4,8},{8,12},{12,16},{16,20},{20,24},{24,28},{1,5},{5,9},{9,... | collective-permute-start | bytes 786440 | tf_op jit(solution)/shard_map/ppermute | solution.py:17
  39.2 1.5 %collective-permute-start.4 = (f32[2,1,128,256]{3,0,2,1:T(2,128)S(1)}, f32[2,1,128,256]{3,0,2,1:T(2,128)S(1)}, u32[]{:S(2)}, u32[]{:S(2)}) collective-permute-start(f32[2,1,128,256]{3,0,2,1:T(2,128)S(1)} %get-tuple-element.195), channel_id=1, source_target_pairs={{4,0},{8,4},{12,8},{16,12},{20,16},{24,20},{28,24},{5,1},{9,5},{13... | collective-permute-start | bytes 786440 | tf_op jit(solution)/shard_map/ppermute | solution.py:20
  40.7 3.2 %collective-permute-done.3 = f32[2,1,128,256]{3,0,2,1:T(2,128)S(1)} collective-permute-done((f32[2,1,128,256]{3,0,2,1:T(2,128)S(1)}, f32[2,1,128,256]{3,0,2,1:T(2,128)S(1)}, u32[]{:S(2)}, u32[]{:S(2)}) %collective-permute-start.3) | collective-permute-done | bytes 262176 | tf_op jit(solution)/shard_map/ppermute | solution.py:17
  43.9 5.9 %collective-permute-done.4 = f32[2,1,128,256]{3,0,2,1:T(2,128)S(1)} collective-permute-done((f32[2,1,128,256]{3,0,2,1:T(2,128)S(1)}, f32[2,1,128,256]{3,0,2,1:T(2,128)S(1)}, u32[]{:S(2)}, u32[]{:S(2)}) %collective-permute-start.4) | collective-permute-done | bytes 262176 | tf_op jit(solution)/shard_map/ppermute | solution.py:20
  49.8 0.5 pad_maximum_fusion.1
  50.4 0.7 fusion.28
  51.1 0.3 fusion.26
  51.4 0.3 fusion.27
  51.8 3.2 %fusion.23 = (bf16[2,128,256]{2,1,0:T(8,128)(2,1)}, f32[2,2,128,256]{3,0,2,1:T(2,128)S(1)}) fusion(f32[2,2,128,1]{3,0,2,1:T(2,128)S(1)} %get-tuple-element.183, f32[2,2,128,255]{3,0,2,1:T(2,128)S(1)} %get-tuple-element.185, f32[2,2,128,255]{3,0,2,1:T(2,128)S(1)} %get-tuple-element.184, f32[2,2,128,1]{3,0,2,1:T(2,128)S(1)} %get-tuple-element.182, ...), kind=kLoop, calls=%fused_computation.46 | loop fusion | flops 2293760 | bytes 4849664 | tf_op jit(solution)/shard_map/reduce_sum | solution.py:72
  55.0 35.5 %all-reduce.2.cloned.1.call-done = bf16[2,128,256]{2,1,0:T(8,128)(2,1)} async-done(((bf16[2,128,256]{2,1,0:T(8,128)(2,1)}), bf16[2,128,256]{2,1,0:T(8,128)(2,1)}) %all-reduce.2.cloned.1.call-update) | async-done | bytes 131088 | tf_op jit(solution)/shard_map/psum | solution.py:74
  90.4 0.9 convert_multiply_fusion
  91.4 0.3 subtract_convert_fusion
  91.7 0.9 convolution_bitcast_fusion
  92.5 0.2 copy.52
  92.9 21.1 %while.19 = (s32[]{:T(128)}, f32[2,8]{1,0:T(2,128)S(1)}, bf16[2,65536]{1,0:T(2,128)(2,1)S(1)}, bf16[2,65536]{1,0:T(2,128)(2,1)S(1)}, s32[]{:T(128)}, /*index=5*/...) while((s32[]{:T(128)}, f32[2,8]{1,0:T(2,128)S(1)}, ...), condition=%wide.region_3.4_spmd, body=%wide.region_2.3_spmd.sunk | while | flops 524306 | bytes 2097520 | solution.py:101
  93.0 5.8 %collective-permute-done = bf16[2,65536]{1,0:T(2,128)(2,1)S(1)} collective-permute-done((bf16[2,65536]{1,0:T(2,128)(2,1)S(1)}, bf16[2,65536]{1,0:T(2,128)(2,1)S(1)}, u32[]{:S(2)}, u32[]{:S(2)}) %collective-permute-start) | collective-permute-done | bytes 262176 | tf_op jit(solution)/shard_map/while/body/eval_jaxpr/ppermute | solution.py:28
  98.8 0.8 fusion.45
  99.5 0.2 dynamic_update_slice.15
  99.7 0.2 copy.58
  100.0 5.8 %collective-permute-done = bf16[2,65536]{1,0:T(2,128)(2,1)S(1)} collective-permute-done((bf16[2,65536]{1,0:T(2,128)(2,1)S(1)}, bf16[2,65536]{1,0:T(2,128)(2,1)S(1)}, u32[]{:S(2)}, u32[]{:S(2)}) %collective-permute-start) | collective-permute-done | bytes 262176 | tf_op jit(solution)/shard_map/while/body/eval_jaxpr/ppermute | solution.py:28
  105.8 0.8 fusion.45
  106.7 0.2 copy.58
  107.1 5.8 %collective-permute-done = bf16[2,65536]{1,0:T(2,128)(2,1)S(1)} collective-permute-done((bf16[2,65536]{1,0:T(2,128)(2,1)S(1)}, bf16[2,65536]{1,0:T(2,128)(2,1)S(1)}, u32[]{:S(2)}, u32[]{:S(2)}) %collective-permute-start) | collective-permute-done | bytes 262176 | tf_op jit(solution)/shard_map/while/body/eval_jaxpr/ppermute | solution.py:28
  112.8 0.8 fusion.45
  113.6 0.2 dynamic_update_slice.15
  113.8 0.2 copy.58
  114.0 1.5 %collective-permute-start.5 = (f32[2,8]{1,0:T(2,128)S(1)}, f32[2,8]{1,0:T(2,128)S(1)}, u32[]{:S(2)}, u32[]{:S(2)}) collective-permute-start(f32[2,8]{1,0:T(2,128)S(1)} %broadcast_multiply_fusion), channel_id=1, source_target_pairs={{0,4},{4,0},{8,12},{12,8},{16,20},{20,16},{24,28},{28,24},{1,5},{5... | collective-permute-start | bytes 200 | tf_op jit(solution)/shard_map/ppermute | solution.py:105
  115.5 2.1 %collective-permute-done.5 = f32[2,8]{1,0:T(2,128)S(1)} collective-permute-done((f32[2,8]{1,0:T(2,128)S(1)}, f32[2,8]{1,0:T(2,128)S(1)}, u32[]{:S(2)}, u32[]{:S(2)}) %collective-permute-start.5) | collective-permute-done | bytes 96 | tf_op jit(solution)/shard_map/ppermute | solution.py:105
  117.6 1.5 %collective-permute-start.6 = (f32[2,8]{1,0:T(2,128)S(1)}, f32[2,8]{1,0:T(2,128)S(1)}, u32[]{:S(2)}, u32[]{:S(2)}) collective-permute-start(f32[2,8]{1,0:T(2,128)S(1)} %fusion.22), channel_id=1, source_target_pairs={{0,8},{4,12},{8,0},{12,4},{16,24},{20,28},{24,16},{28,20},{1,9},{5... | collective-permute-start | bytes 200 | tf_op jit(solution)/shard_map/ppermute | solution.py:105
  119.1 2.1 %collective-permute-done.6 = f32[2,8]{1,0:T(2,128)S(1)} collective-permute-done((f32[2,8]{1,0:T(2,128)S(1)}, f32[2,8]{1,0:T(2,128)S(1)}, u32[]{:S(2)}, u32[]{:S(2)}) %collective-permute-start.6) | collective-permute-done | bytes 96 | tf_op jit(solution)/shard_map/ppermute | solution.py:105
  121.2 2.4 %collective-permute-start.7 = (f32[2,8]{1,0:T(2,128)S(1)}, f32[2,8]{1,0:T(2,128)S(1)}, u32[]{:S(2)}, u32[]{:S(2)}) collective-permute-start(f32[2,8]{1,0:T(2,128)S(1)} %add.129), channel_id=1, source_target_pairs={{0,16},{4,20},{8,24},{12,28},{16,0},{20,4},{24,8},{28,12},{1,17},{... | collective-permute-start | bytes 200 | tf_op jit(solution)/shard_map/ppermute | solution.py:105
  123.6 0.8 copy.32
  124.5 1.2 collective-permute-done.7
  125.7 5.1 %all-gather = f32[4,2,8]{2,1,0:T(2,128)S(1)} all-gather(f32[1,2,8]{2,1,0:T(2,128)S(1)} %add_bitcast_fusion), channel_id=1, replica_groups=mesh['space'=8,'member'=4] {'member'}, dimensions={0}, use_global_device_ids=true | all-gather | bytes 320 | tf_op jit(solution)/shard_map/all_gather | solution.py:106
  130.9 0.7 cholesky.19
  131.8 0.7 compare_reduce_fusion
  132.5 1.2 select_bitcast_fusion
  (28 shorter events, 1.5 us)
Async XLA Ops:
  7.2 18.2 %copy-start.1 = (s32[2]{0:T(128)S(1)}, s32[2]{0:T(128)}, u32[]{:S(2)}) copy-start(s32[2]{0:T(128)} %param.15) | copy-start | bytes 28
  7.2 83.3 %all-reduce.2.cloned.1.call-start = ((), (), s32[]{:S(2)}) async-start(), calls=%async_computation | async-start | bytes 262144 | tf_op jit(solution)/shard_map/psum | solution.py:74
  8.9 16.0 %collective-permute-start.1 = (f32[2,1,128,256]{3,0,2,1:T(2,128)S(1)}, f32[2,1,128,256]{3,0,2,1:T(2,128)S(1)}, u32[]{:S(2)}, u32[]{:S(2)}) collective-permute-start(f32[2,1,128,256]{3,0,2,1:T(2,128)S(1)} %get-tuple-element.196), channel_id=1, source_target_pairs={{0,4},{4,8},{8,12},{12,16},{16,20},{20,24},{24,28},{1,5},{5,9},{9,... | collective-permute-start | bytes 786440 | tf_op jit(solution)/shard_map/ppermute | solution.py:17
  13.7 11.2 %collective-permute-start.2 = (f32[2,1,128,256]{3,0,2,1:T(2,128)S(1)}, f32[2,1,128,256]{3,0,2,1:T(2,128)S(1)}, u32[]{:S(2)}, u32[]{:S(2)}) collective-permute-start(f32[2,1,128,256]{3,0,2,1:T(2,128)S(1)} %get-tuple-element.197), channel_id=1, source_target_pairs={{4,0},{8,4},{12,8},{16,12},{20,16},{24,20},{28,24},{5,1},{9,5},{13... | collective-permute-start | bytes 786440 | tf_op jit(solution)/shard_map/ppermute | solution.py:20
  25.4 7.3 %copy-start = (f32[2,128,256]{2,1,0:T(8,128)S(1)}, f32[2,128,256]{2,1,0:T(8,128)}, u32[]{:S(2)}) copy-start(f32[2,128,256]{2,1,0:T(8,128)} %param.12) | copy-start | bytes 786436
  34.8 9.1 %collective-permute-start.3 = (f32[2,1,128,256]{3,0,2,1:T(2,128)S(1)}, f32[2,1,128,256]{3,0,2,1:T(2,128)S(1)}, u32[]{:S(2)}, u32[]{:S(2)}) collective-permute-start(f32[2,1,128,256]{3,0,2,1:T(2,128)S(1)} %get-tuple-element.194), channel_id=1, source_target_pairs={{0,4},{4,8},{8,12},{12,16},{16,20},{20,24},{24,28},{1,5},{5,9},{9,... | collective-permute-start | bytes 786440 | tf_op jit(solution)/shard_map/ppermute | solution.py:17
  39.2 10.5 %collective-permute-start.4 = (f32[2,1,128,256]{3,0,2,1:T(2,128)S(1)}, f32[2,1,128,256]{3,0,2,1:T(2,128)S(1)}, u32[]{:S(2)}, u32[]{:S(2)}) collective-permute-start(f32[2,1,128,256]{3,0,2,1:T(2,128)S(1)} %get-tuple-element.195), channel_id=1, source_target_pairs={{4,0},{8,4},{12,8},{16,12},{20,16},{24,20},{28,24},{5,1},{9,5},{13... | collective-permute-start | bytes 786440 | tf_op jit(solution)/shard_map/ppermute | solution.py:20
  92.9 5.8 %collective-permute-start = (bf16[2,65536]{1,0:T(2,128)(2,1)S(1)}, bf16[2,65536]{1,0:T(2,128)(2,1)S(1)}, u32[]{:S(2)}, u32[]{:S(2)}) collective-permute-start(bf16[2,65536]{1,0:T(2,128)(2,1)S(1)} %get-tuple-element.244), channel_id=1, source_target_pairs={{3,0},{0,1},{1,2},{2,3},{7,4},{4,5},{5,6},{6,7},{11,8},{8,9},{9,10... | collective-permute-start | bytes 786440 | tf_op jit(solution)/shard_map/while/body/eval_jaxpr/ppermute | solution.py:28
  99.9 5.8 %collective-permute-start = (bf16[2,65536]{1,0:T(2,128)(2,1)S(1)}, bf16[2,65536]{1,0:T(2,128)(2,1)S(1)}, u32[]{:S(2)}, u32[]{:S(2)}) collective-permute-start(bf16[2,65536]{1,0:T(2,128)(2,1)S(1)} %get-tuple-element.244), channel_id=1, source_target_pairs={{3,0},{0,1},{1,2},{2,3},{7,4},{4,5},{5,6},{6,7},{11,8},{8,9},{9,10... | collective-permute-start | bytes 786440 | tf_op jit(solution)/shard_map/while/body/eval_jaxpr/ppermute | solution.py:28
  107.0 5.8 %collective-permute-start = (bf16[2,65536]{1,0:T(2,128)(2,1)S(1)}, bf16[2,65536]{1,0:T(2,128)(2,1)S(1)}, u32[]{:S(2)}, u32[]{:S(2)}) collective-permute-start(bf16[2,65536]{1,0:T(2,128)(2,1)S(1)} %get-tuple-element.244), channel_id=1, source_target_pairs={{3,0},{0,1},{1,2},{2,3},{7,4},{4,5},{5,6},{6,7},{11,8},{8,9},{9,10... | collective-permute-start | bytes 786440 | tf_op jit(solution)/shard_map/while/body/eval_jaxpr/ppermute | solution.py:28
  114.0 3.6 %collective-permute-start.5 = (f32[2,8]{1,0:T(2,128)S(1)}, f32[2,8]{1,0:T(2,128)S(1)}, u32[]{:S(2)}, u32[]{:S(2)}) collective-permute-start(f32[2,8]{1,0:T(2,128)S(1)} %broadcast_multiply_fusion), channel_id=1, source_target_pairs={{0,4},{4,0},{8,12},{12,8},{16,20},{20,16},{24,28},{28,24},{1,5},{5... | collective-permute-start | bytes 200 | tf_op jit(solution)/shard_map/ppermute | solution.py:105
  117.6 3.6 %collective-permute-start.6 = (f32[2,8]{1,0:T(2,128)S(1)}, f32[2,8]{1,0:T(2,128)S(1)}, u32[]{:S(2)}, u32[]{:S(2)}) collective-permute-start(f32[2,8]{1,0:T(2,128)S(1)} %fusion.22), channel_id=1, source_target_pairs={{0,8},{4,12},{8,0},{12,4},{16,24},{20,28},{24,16},{28,20},{1,9},{5... | collective-permute-start | bytes 200 | tf_op jit(solution)/shard_map/ppermute | solution.py:105
  121.2 4.5 %collective-permute-start.7 = (f32[2,8]{1,0:T(2,128)S(1)}, f32[2,8]{1,0:T(2,128)S(1)}, u32[]{:S(2)}, u32[]{:S(2)}) collective-permute-start(f32[2,8]{1,0:T(2,128)S(1)} %add.129), channel_id=1, source_target_pairs={{0,16},{4,20},{8,24},{12,28},{16,0},{20,4},{24,8},{28,12},{1,17},{... | collective-permute-start | bytes 200 | tf_op jit(solution)/shard_map/ppermute | solution.py:105
Sparse Core Ops, SparseCore 0:
  55.1 35.3 all-reduce.1
